TPU v7x, 32 devices: a whole 2x2x4 slice. The times are simulated.
32 devices in a mesh: ctx: 8 (over z, y), fsdp: 4 (over x, core).
Axes of the slice: x: 2, y: 2, z: 4, core: 2. Of those that a mesh axis runs over, the one named last changes fastest.
Arguments:
- inputs: bfloat16 [16, 1024, 640], P('fsdp', 'ctx'), may hold values from -6 to 6
- cotangent: bfloat16 [16, 1024, 640], P('fsdp', 'ctx'), may hold values from -6 to 6
- lengths: int32 [16], P('fsdp'), may hold values from 256 to 1024, as said below
- query_weight: bfloat16 [640, 1024], P('fsdp'), may hold values from -0.25 to 0.25
- key_weight: bfloat16 [640, 256], P('fsdp'), may hold values from -0.25 to 0.25
- value_weight: bfloat16 [640, 256], P('fsdp'), may hold values from -0.25 to 0.25
- out_weight: bfloat16 [1024, 640], P('fsdp'), may hold values from -0.1875 to 0.1875
- gate_weight: bfloat16 [640, 2048], P('fsdp'), may hold values from -0.25 to 0.25
- up_weight: bfloat16 [640, 2048], P('fsdp'), may hold values from -0.25 to 0.25
- down_weight: bfloat16 [2048, 640], P('fsdp'), may hold values from -0.125 to 0.125
- pre_attn_gain: bfloat16 [640], P('fsdp'), may hold values from -0.5 to 0.5
- post_attn_gain: bfloat16 [640], P('fsdp'), may hold values from -0.5 to 0.5
- pre_ffw_gain: bfloat16 [640], P('fsdp'), may hold values from -0.5 to 0.5
- post_ffw_gain: bfloat16 [640], P('fsdp'), may hold values from -0.5 to 0.5
- query_gain: bfloat16 [256], P('fsdp'), may hold values from 0 to 0.796875
- key_gain: bfloat16 [256], P('fsdp'), may hold values from 0 to 0.796875
Outputs:
- outputs: bfloat16 [16, 1024, 640], P('fsdp', 'ctx')
- input_grad: bfloat16 [16, 1024, 640], P('fsdp', 'ctx')
- query_weight_grad: float32 [640, 1024], P('fsdp')
- key_weight_grad: float32 [640, 256], P('fsdp')
- value_weight_grad: float32 [640, 256], P('fsdp')
- out_weight_grad: float32 [1024, 640], P('fsdp')
- gate_weight_grad: float32 [640, 2048], P('fsdp')
- up_weight_grad: float32 [640, 2048], P('fsdp')
- down_weight_grad: float32 [2048, 640], P('fsdp')
- pre_attn_gain_grad: float32 [640], P('fsdp')
- post_attn_gain_grad: float32 [640], P('fsdp')
- pre_ffw_gain_grad: float32 [640], P('fsdp')
- post_ffw_gain_grad: float32 [640], P('fsdp')
- query_gain_grad: float32 [256], P('fsdp')
- key_gain_grad: float32 [256], P('fsdp')
Inputs may be any that keep to these rules, and one draw needn't show every extreme that they name: Sequence s has its first lengths[s] positions live; later keys are excluded from every softmax. In each aligned block of 4 sequences exactly one, drawn from the seed, has all 1024 positions live.
All inputs are finite; a program needn't handle non-finite values.
Results may differ from a plain program's by a relative error of at most 0.022.
Values may be sent and summed in bfloat16 or wider, within the bound.
A program may use at most 256 MiB of HBM per device.

v0:
```python
import math
import jax
import jax.numpy as jnp
from jax import lax
from jax.sharding import PartitionSpec as P

EPSILON = 1e-06
MASKED_SCORE = -1e30
ROPE_BASE = 1000000.0


def norm_gain(values, gain_vec):
    return (
        values
        * lax.rsqrt(jnp.mean(values * values, axis=-1, keepdims=True) + EPSILON)
        * (1.0 + gain_vec)
    )


def rotate(values, positions):
    half_dim = values.shape[-1] // 2
    inverse = ROPE_BASE ** (-(jnp.arange(half_dim).astype(jnp.float32) * 2.0) / values.shape[-1])
    angles = positions.astype(jnp.float32)[:, None] * inverse[None, :]
    cosine = jnp.cos(angles)[:, None, :]
    sine_part = jnp.sin(angles)[:, None, :]
    first_half = values[..., :half_dim]
    second_half = values[..., half_dim:]
    return jnp.concatenate(
        [
            first_half * cosine - second_half * sine_part,
            second_half * cosine + first_half * sine_part,
        ],
        axis=-1,
    )


def gelu_mix(gate_in, up_in):
    return jax.nn.gelu(gate_in, approximate=True) * up_in


def body(
    inputs,
    cotangent,
    lengths,
    query_weight,
    key_weight,
    value_weight,
    out_weight,
    gate_weight,
    up_weight,
    down_weight,
    pre_attn_gain,
    post_attn_gain,
    pre_ffw_gain,
    post_ffw_gain,
    query_gain,
    key_gain,
):
    seq_count, row_count, model_width = inputs.shape
    gathered = (
        lax.all_gather(query_weight, "fsdp", axis=0, tiled=True),
        lax.all_gather(key_weight, "fsdp", axis=0, tiled=True),
        lax.all_gather(value_weight, "fsdp", axis=0, tiled=True),
        lax.all_gather(out_weight, "fsdp", axis=0, tiled=True),
        lax.all_gather(gate_weight, "fsdp", axis=0, tiled=True),
        lax.all_gather(up_weight, "fsdp", axis=0, tiled=True),
        lax.all_gather(down_weight, "fsdp", axis=0, tiled=True),
        lax.all_gather(pre_attn_gain, "fsdp", axis=0, tiled=True),
        lax.all_gather(post_attn_gain, "fsdp", axis=0, tiled=True),
        lax.all_gather(pre_ffw_gain, "fsdp", axis=0, tiled=True),
        lax.all_gather(post_ffw_gain, "fsdp", axis=0, tiled=True),
        lax.all_gather(query_gain, "fsdp", axis=0, tiled=True),
        lax.all_gather(key_gain, "fsdp", axis=0, tiled=True),
    )
    (
        query_full,
        key_full,
        value_full,
        out_full,
        gate_full,
        up_full,
        down_full,
        gain_attn_in,
        gain_attn_out,
        gain_ffw_in,
        gain_ffw_out,
        gain_query,
        gain_key,
    ) = gathered
    gain_attn_in = gain_attn_in.astype(jnp.float32)
    gain_attn_out = gain_attn_out.astype(jnp.float32)
    gain_ffw_in = gain_ffw_in.astype(jnp.float32)
    gain_ffw_out = gain_ffw_out.astype(jnp.float32)
    gain_query = gain_query.astype(jnp.float32)
    gain_key = gain_key.astype(jnp.float32)
    head_dim = key_full.shape[1]
    head_count = query_full.shape[1] // head_dim
    seq_len = row_count * lax.axis_size("ctx")
    key_span = math.gcd(512, seq_len)
    att_scale = head_dim ** (-0.5)
    flat_rows = seq_count * row_count
    positions = lax.axis_index("ctx") * row_count + jnp.arange(row_count, dtype=jnp.int32)
    x_flat = inputs.astype(jnp.float32).reshape(flat_rows, model_width)
    attn_in, attn_in_back = jax.vjp(norm_gain, x_flat, gain_attn_in)
    attn_in_b = attn_in.astype(jnp.bfloat16)
    query_lin = jnp.dot(attn_in_b, query_full, preferred_element_type=jnp.float32)
    key_lin = jnp.dot(attn_in_b, key_full, preferred_element_type=jnp.float32)
    value_lin = jnp.dot(attn_in_b, value_full, preferred_element_type=jnp.float32)

    def query_side(lin_values, gain_vec):
        return rotate(
            norm_gain(lin_values.reshape(seq_count, row_count, head_count, head_dim), gain_vec),
            positions,
        )

    def key_side(lin_values, gain_vec):
        return rotate(
            norm_gain(lin_values.reshape(seq_count, row_count, 1, head_dim), gain_vec), positions
        )[:, :, 0, :]

    query_rot, query_side_back = jax.vjp(query_side, query_lin, gain_query)
    key_rot, key_side_back = jax.vjp(key_side, key_lin, gain_key)
    query_b = query_rot.astype(jnp.bfloat16)
    key_b = key_rot.astype(jnp.bfloat16)
    value_b = value_lin.reshape(seq_count, row_count, head_dim).astype(jnp.bfloat16)

    def allowed(key_begin, key_count):
        key_pos = key_begin + jnp.arange(key_count, dtype=jnp.int32)
        causal = key_pos[None, :] <= positions[:, None]
        live = key_pos[None, :] < lengths[:, None]
        return (causal[None] & live[:, None, :])[:, None]

    def raw_scores(key_piece):
        return (
            jnp.einsum("sqhd,skd->shqk", query_b, key_piece, preferred_element_type=jnp.float32)
            * att_scale
        )

    stat_shape = (seq_count, head_count, row_count)
    running_max = jnp.full(stat_shape, MASKED_SCORE, jnp.float32)
    key_piece = lax.all_gather(key_b, "ctx", axis=1, tiled=True)
    value_piece = lax.all_gather(value_b, "ctx", axis=1, tiled=True)
    mask_now = allowed(jnp.int32(0), key_piece.shape[1])
    scores = jnp.where(mask_now, raw_scores(key_piece), MASKED_SCORE)
    new_max = jnp.maximum(running_max, jnp.max(scores, axis=-1))
    weights = jnp.where(mask_now, jnp.exp(scores - new_max[..., None]), 0.0)
    new_sum = jnp.sum(weights, axis=-1)
    new_acc = jnp.einsum(
        "shqk,skd->shqd",
        weights.astype(jnp.bfloat16),
        value_piece,
        preferred_element_type=jnp.float32,
    )
    final_state = (new_max, new_sum, new_acc)
    final_max, final_sum, final_acc = final_state
    attended = final_acc / final_sum[..., None]
    log_total = final_max + jnp.log(final_sum)
    attended_b = (
        attended.transpose(0, 2, 1, 3)
        .reshape(flat_rows, head_count * head_dim)
        .astype(jnp.bfloat16)
    )
    attn_lin = jnp.dot(attended_b, out_full, preferred_element_type=jnp.float32)
    attn_post, attn_post_back = jax.vjp(norm_gain, attn_lin, gain_attn_out)
    middle = x_flat + attn_post
    ffw_in, ffw_in_back = jax.vjp(norm_gain, middle, gain_ffw_in)
    ffw_in_b = ffw_in.astype(jnp.bfloat16)
    gate_lin = jnp.dot(ffw_in_b, gate_full, preferred_element_type=jnp.float32)
    up_lin = jnp.dot(ffw_in_b, up_full, preferred_element_type=jnp.float32)
    hidden, hidden_back = jax.vjp(gelu_mix, gate_lin, up_lin)
    hidden_b = hidden.astype(jnp.bfloat16)
    ffw_out = jnp.dot(hidden_b, down_full, preferred_element_type=jnp.float32)
    ffw_post, ffw_post_back = jax.vjp(norm_gain, ffw_out, gain_ffw_out)
    outputs = (middle + ffw_post).astype(jnp.bfloat16).reshape(seq_count, row_count, model_width)
    grad_top = cotangent.astype(jnp.float32).reshape(flat_rows, model_width)
    d_ffw_out, grad_ffw_out_gain = ffw_post_back(grad_top)
    d_ffw_out_b = d_ffw_out.astype(jnp.bfloat16)
    grad_down = jnp.einsum("rf,rd->fd", hidden_b, d_ffw_out_b, preferred_element_type=jnp.float32)
    d_hidden = jnp.einsum("rd,fd->rf", d_ffw_out_b, down_full, preferred_element_type=jnp.float32)
    d_gate, d_up = hidden_back(d_hidden)
    d_gate_b = d_gate.astype(jnp.bfloat16)
    d_up_b = d_up.astype(jnp.bfloat16)
    grad_gate = jnp.einsum("rd,rf->df", ffw_in_b, d_gate_b, preferred_element_type=jnp.float32)
    grad_up = jnp.einsum("rd,rf->df", ffw_in_b, d_up_b, preferred_element_type=jnp.float32)
    d_ffw_in = jnp.einsum(
        "rf,df->rd", d_gate_b, gate_full, preferred_element_type=jnp.float32
    ) + jnp.einsum("rf,df->rd", d_up_b, up_full, preferred_element_type=jnp.float32)
    d_middle_part, grad_ffw_in_gain = ffw_in_back(d_ffw_in)
    d_middle = grad_top + d_middle_part
    d_attn_lin, grad_attn_out_gain = attn_post_back(d_middle)
    d_attn_b = d_attn_lin.astype(jnp.bfloat16)
    grad_projection = jnp.einsum(
        "ro,rd->od", attended_b, d_attn_b, preferred_element_type=jnp.float32
    )
    d_attended_b = (
        jnp.einsum("rd,od->ro", d_attn_b, out_full, preferred_element_type=jnp.float32)
        .astype(jnp.bfloat16)
        .reshape(seq_count, row_count, head_count, head_dim)
    )
    d_attended = d_attended_b.astype(jnp.float32)
    row_delta = jnp.einsum("sqhd,shqd->shq", d_attended, attended, precision=lax.Precision.HIGHEST)

    def key_grads(key_piece, value_piece, key_begin):
        mask_now = allowed(key_begin, key_piece.shape[1])
        probabilities = jnp.where(
            mask_now, jnp.exp(raw_scores(key_piece) - log_total[..., None]), 0.0
        )
        d_probs = jnp.einsum(
            "sqhd,skd->shqk", d_attended_b, value_piece, preferred_element_type=jnp.float32
        )
        d_scores = (probabilities * (d_probs - row_delta[..., None])).astype(jnp.bfloat16)
        d_query = (
            jnp.einsum("shqk,skd->sqhd", d_scores, key_piece, preferred_element_type=jnp.float32)
            * att_scale
        )
        d_key = (
            jnp.einsum("shqk,sqhd->skd", d_scores, query_b, preferred_element_type=jnp.float32)
            * att_scale
        )
        d_value = jnp.einsum(
            "shqk,sqhd->skd",
            probabilities.astype(jnp.bfloat16),
            d_attended_b,
            preferred_element_type=jnp.float32,
        )
        return (d_query, jnp.concatenate([d_key, d_value], axis=-1))

    key_back_all, value_back_all = (
        lax.all_gather(key_b, "ctx", axis=1, tiled=True),
        lax.all_gather(value_b, "ctx", axis=1, tiled=True),
    )

    def slice_keys(key_begin, key_count):
        return (
            lax.dynamic_slice_in_dim(key_back_all, key_begin, key_count, 1),
            lax.dynamic_slice_in_dim(value_back_all, key_begin, key_count, 1),
        )

    query_zero = jnp.zeros((seq_count, row_count, head_count, head_dim), jnp.float32)

    def joint_step(block_id, state):
        d_query_sum, key_buffer = state
        key_begin = block_id * key_span
        key_piece, value_piece = slice_keys(key_begin, key_span)
        d_query, d_keyval = key_grads(key_piece, value_piece, key_begin)
        return (
            d_query_sum + d_query,
            lax.dynamic_update_slice_in_dim(key_buffer, d_keyval, key_begin, 1),
        )

    d_query_rot, key_buffer = lax.fori_loop(
        0,
        seq_len // key_span,
        joint_step,
        (query_zero, jnp.zeros((seq_count, seq_len, 2 * head_dim), jnp.float32)),
    )
    d_keyval_own = lax.psum_scatter(key_buffer, "ctx", scatter_dimension=1, tiled=True)
    d_key_rot = d_keyval_own[..., :head_dim]
    d_value = d_keyval_own[..., head_dim:]
    d_query_lin, grad_query_gain = query_side_back(d_query_rot)
    d_key_lin, grad_key_gain = key_side_back(d_key_rot)
    d_query_b = d_query_lin.astype(jnp.bfloat16)
    d_key_b = d_key_lin.astype(jnp.bfloat16)
    d_value_b = d_value.reshape(flat_rows, head_dim).astype(jnp.bfloat16)
    grad_query = jnp.einsum("rd,rq->dq", attn_in_b, d_query_b, preferred_element_type=jnp.float32)
    grad_key = jnp.einsum("rd,rq->dq", attn_in_b, d_key_b, preferred_element_type=jnp.float32)
    grad_value = jnp.einsum("rd,rq->dq", attn_in_b, d_value_b, preferred_element_type=jnp.float32)
    d_attn_in = jnp.einsum("rq,dq->rd", d_query_b, query_full, preferred_element_type=jnp.float32)
    d_attn_in = d_attn_in + jnp.einsum(
        "rq,dq->rd", d_key_b, key_full, preferred_element_type=jnp.float32
    )
    d_attn_in = d_attn_in + jnp.einsum(
        "rq,dq->rd", d_value_b, value_full, preferred_element_type=jnp.float32
    )
    d_input_part, grad_attn_in_gain = attn_in_back(d_attn_in)
    input_grad = (
        (d_middle + d_input_part).astype(jnp.bfloat16).reshape(seq_count, row_count, model_width)
    )
    shards = (
        lax.psum_scatter(
            grad_query.astype(jnp.bfloat16), "fsdp", scatter_dimension=0, tiled=True
        ).astype(jnp.float32),
        lax.psum_scatter(
            grad_key.astype(jnp.bfloat16), "fsdp", scatter_dimension=0, tiled=True
        ).astype(jnp.float32),
        lax.psum_scatter(
            grad_value.astype(jnp.bfloat16), "fsdp", scatter_dimension=0, tiled=True
        ).astype(jnp.float32),
        lax.psum_scatter(
            grad_projection.astype(jnp.bfloat16), "fsdp", scatter_dimension=0, tiled=True
        ).astype(jnp.float32),
        lax.psum_scatter(
            grad_gate.astype(jnp.bfloat16), "fsdp", scatter_dimension=0, tiled=True
        ).astype(jnp.float32),
        lax.psum_scatter(
            grad_up.astype(jnp.bfloat16), "fsdp", scatter_dimension=0, tiled=True
        ).astype(jnp.float32),
        lax.psum_scatter(
            grad_down.astype(jnp.bfloat16), "fsdp", scatter_dimension=0, tiled=True
        ).astype(jnp.float32),
        lax.psum_scatter(
            grad_attn_in_gain.astype(jnp.bfloat16), "fsdp", scatter_dimension=0, tiled=True
        ).astype(jnp.float32),
        lax.psum_scatter(
            grad_attn_out_gain.astype(jnp.bfloat16), "fsdp", scatter_dimension=0, tiled=True
        ).astype(jnp.float32),
        lax.psum_scatter(
            grad_ffw_in_gain.astype(jnp.bfloat16), "fsdp", scatter_dimension=0, tiled=True
        ).astype(jnp.float32),
        lax.psum_scatter(
            grad_ffw_out_gain.astype(jnp.bfloat16), "fsdp", scatter_dimension=0, tiled=True
        ).astype(jnp.float32),
        lax.psum_scatter(
            grad_query_gain.astype(jnp.bfloat16), "fsdp", scatter_dimension=0, tiled=True
        ).astype(jnp.float32),
        lax.psum_scatter(
            grad_key_gain.astype(jnp.bfloat16), "fsdp", scatter_dimension=0, tiled=True
        ).astype(jnp.float32),
    )
    totals = lax.psum(
        (
            shards[0],
            shards[1],
            shards[2],
            shards[3],
            shards[4],
            shards[5],
            shards[6],
            shards[7],
            shards[8],
            shards[9],
            shards[10],
            shards[11],
            shards[12],
        ),
        "ctx",
    )
    return (outputs, input_grad) + tuple(totals)


def solution(mesh):
    in_specs = (
        P("fsdp", "ctx", None),
        P("fsdp", "ctx", None),
        P("fsdp"),
        P("fsdp", None),
        P("fsdp", None),
        P("fsdp", None),
        P("fsdp", None),
        P("fsdp", None),
        P("fsdp", None),
        P("fsdp", None),
        P("fsdp"),
        P("fsdp"),
        P("fsdp"),
        P("fsdp"),
        P("fsdp"),
        P("fsdp"),
    )
    out_specs = (
        P("fsdp", "ctx", None),
        P("fsdp", "ctx", None),
        P("fsdp", None),
        P("fsdp", None),
        P("fsdp", None),
        P("fsdp", None),
        P("fsdp", None),
        P("fsdp", None),
        P("fsdp", None),
        P("fsdp"),
        P("fsdp"),
        P("fsdp"),
        P("fsdp"),
        P("fsdp"),
        P("fsdp"),
    )
    return jax.shard_map(body, mesh=mesh, in_specs=in_specs, out_specs=out_specs, check_vma=False)
```

profile of v0, /device:TPU:0, one launch (start us, length us, event | category | flops | bytes accessed | tf_op | source)
XLA Modules:
  0.0 893.9 jit_solution(16385621297810421104)
XLA Ops:
  8.0 1.3 fusion.76
  17.0 9.2 %all-reduce.18 = (bf16[256]{0:T(256)(128)(2,1)S(1)}, bf16[640]{0:T(1024)(128)(2,1)S(1)}, bf16[256]{0:T(256)(128)(2,1)S(1)}, bf16[640]{0:T(1024)(128)(2,1)S(1)}, ...) all-reduce(bf16[256]{0:T(256)(128)(2,1)S(1)} %dynamic-update-slice., ...), channel_id=1, replica_groups=mesh['ctx'=8,'fsdp'=4] {'fsdp'}, use_global_device_ids=true, to_apply=%add.5 | all-reduce | flops 3072 | bytes 12288
  26.3 6.2 all_gather.48
  32.5 1.4 fusion.56
  36.3 6.2 all_gather.53
  46.7 1.9 broadcast_and_fusion.1
  48.5 2.4 copy.67
  50.9 2.4 multiply_reduce_fusion.3
  57.1 1.6 copy.70
  58.8 27.3 %all-gather.21.cloned.1.call-done = bf16[4,1024,1,256]{3,1,0,2:T(8,128)(2,1)} async-done(((bf16[4,128,1,256]{3,1,0,2:T(8,128)(2,1)}), bf16[4,1024,1,256]{3,1,0,2:T(8,128)(2,1)}) %all-gather.21.cloned.1.call-update) | async-done | bytes 2097168 | tf_op jit(solution)/shard_map/all_gather | solution.py:141
  86.0 3.3 fusion.28
  89.4 3.2 copy-done.16
  92.7 2.2 fusion.29
  94.9 41.7 %all-gather.11.cloned.1.call-done = bf16[4,1024,256]{2,1,0:T(8,128)(2,1)} async-done(((bf16[4,128,256]{2,1,0:T(8,128)(2,1)}), bf16[4,1024,256]{2,1,0:T(8,128)(2,1)}) %all-gather.11.cloned.1.call-update) | async-done | bytes 2097168 | tf_op jit(solution)/shard_map/all_gather | solution.py:142
  136.6 8.1 fusion.45
  146.8 8.0 all-gather.13.cloned.1.call-done
  154.7 2.8 multiply_reduce_fusion.10
  160.6 21.1 %all-gather.15.cloned.1.call-done = bf16[640,2048]{1,0:T(8,128)(2,1)} async-done(((bf16[160,2048]{1,0:T(8,128)(2,1)}), bf16[640,2048]{1,0:T(8,128)(2,1)}) %all-gather.15.cloned.1.call-update) | async-done | bytes 2621456 | tf_op jit(solution)/shard_map/all_gather | solution.py:65
  181.7 5.8 fusion.78
  187.5 21.2 %all-gather.17.cloned.1.call-done = bf16[640,2048]{1,0:T(8,128)(2,1)} async-done(((bf16[160,2048]{1,0:T(8,128)(2,1)}), bf16[640,2048]{1,0:T(8,128)(2,1)}) %all-gather.17.cloned.1.call-update) | async-done | bytes 2621456 | tf_op jit(solution)/shard_map/all_gather | solution.py:66
  208.7 8.3 multiply_convert_fusion.1
  217.0 18.9 %all-gather.19.cloned.1.call-done = bf16[2048,640]{1,0:T(8,128)(2,1)} async-done(((bf16[512,640]{1,0:T(8,128)(2,1)}), bf16[2048,640]{1,0:T(8,128)(2,1)}) %all-gather.19.cloned.1.call-update) | async-done | bytes 2621456 | tf_op jit(solution)/shard_map/all_gather | solution.py:67
  235.9 4.4 multiply_reduce_fusion.8
  241.6 1.4 fusion.49
  243.6 4.8 multiply_convert_fusion
  248.5 1.8 fusion.79
  251.7 2.1 multiply_reduce_fusion.4
  256.6 2.1 convolution_convert_fusion.3
  258.7 3.5 convolution_convert_fusion.5
  262.2 2.6 reshape.457
  264.8 2.4 copy.71
  267.2 2.9 bitcast_convert_fusion
  270.3 3.0 multiply_reduce_fusion
  273.3 4.3 broadcast_in_dim.140.clone
  277.6 40.3 %while.16 = (s32[]{:T(128)}, f32[4,128,4,256]{1,3,2,0:T(8,128)S(1)}, f32[4,1024,512]{2,1,0:T(8,128)}, bf16[4,1024,256]{2,1,0:T(8,128)(2,1)}, s32[4]{0:T(128)S(1)...) while((s32[]{:T(128)}, ...), condition=%wide.region_12.13_spmd.clone, body=%wide.region_11.12_spmd.clone.sunk | while | flops 2698316288 | bytes 81694016 | solution.py:251
  278.6 2.1 fusion.149
  280.9 1.4 fusion.150
  285.7 2.4 pad_maximum_fusion.5
  288.1 5.3 copy.128
  293.4 4.6 constant_dynamic-update-slice_fusion.2
  298.6 2.1 fusion.149
  300.8 1.4 fusion.150
  305.6 2.4 pad_maximum_fusion.5
  308.0 5.3 copy.128
  313.3 4.6 constant_dynamic-update-slice_fusion.2
  318.0 1.8 copy.72
  319.8 2.0 multiply_add_fusion.1
  325.6 1.9 convolution_convert_fusion.4
  327.6 4.6 convolution_convert_fusion.2
  332.5 4.8 convolution_convert_fusion.1
  338.3 4.9 convolution_convert_fusion
  345.4 3.3 fusion.80
  348.7 5.6 reduce-scatter.11.cloned.1.call-done
  354.4 37.1 %reduce-scatter.19.cloned.1.call-done = bf16[160,2048]{1,0:T(8,128)(2,1)} async-done(((bf16[640,2048]{1,0:T(8,128)(2,1)}), bf16[160,2048]{1,0:T(8,128)(2,1)}) %reduce-scatter.19.cloned.1.call-update) | async-done | bytes 655376 | tf_op jit(solution)/shard_map/reduce_scatter | solution.py:292
  391.5 37.4 %reduce-scatter.21.cloned.1.call-done = bf16[160,2048]{1,0:T(8,128)(2,1)} async-done(((bf16[640,2048]{1,0:T(8,128)(2,1)}), bf16[160,2048]{1,0:T(8,128)(2,1)}) %reduce-scatter.21.cloned.1.call-update) | async-done | bytes 655376 | tf_op jit(solution)/shard_map/reduce_scatter | solution.py:295
  428.9 37.1 %reduce-scatter.23.cloned.1.call-done = bf16[512,640]{1,0:T(8,128)(2,1)} async-done(((bf16[2048,640]{1,0:T(8,128)(2,1)}), bf16[512,640]{1,0:T(8,128)(2,1)}) %reduce-scatter.23.cloned.1.call-update) | async-done | bytes 655376 | tf_op jit(solution)/shard_map/reduce_scatter | solution.py:298
  466.0 153.5 %reduce-scatter.9.cloned.1.call-done = f32[4,128,512]{2,1,0:T(8,128)} async-done(((f32[4,1024,512]{2,1,0:T(8,128)}), f32[4,128,512]{2,1,0:T(8,128)}) %reduce-scatter.9.cloned.1.call-update) | async-done | bytes 1048592 | tf_op jit(solution)/shard_map/reduce_scatter | solution.py:257
  622.6 1.8 convolution_add_fusion.1
  625.6 1.6 fusion.57
  627.2 7.1 all-reduce.17
  635.9 2.7 fusion.52
  638.6 3.3 reduce-scatter.15.cloned.1.call-done
  641.9 23.6 %reduce-scatter.13.cloned.1.call-done = bf16[160,256]{1,0:T(8,128)(2,1)} async-done(((bf16[640,256]{1,0:T(8,128)(2,1)}), bf16[160,256]{1,0:T(8,128)(2,1)}) %reduce-scatter.13.cloned.1.call-update) | async-done | bytes 81936 | tf_op jit(solution)/shard_map/reduce_scatter | solution.py:283
  665.5 221.7 %all-reduce.20 = (f32[160,1024]{1,0:T(8,128)}, f32[160,256]{1,0:T(8,128)}, f32[160,256]{1,0:T(8,128)}, f32[256,640]{1,0:T(8,128)}, f32[160,2048]{1,0:T(8,128)}, ...) all-reduce(bf16[160,1024]{1,0:T(8,128)(2,1)} %reduce-scatter.11.clo, ...), channel_id=1, replica_groups=mesh['ctx'=8,'fsdp'=4] {'ctx'}, use_global_device_ids=true, to_apply=%region_18.19 | all-reduce | flops 1393408 | bytes 8361984 | tf_op jit(solution)/shard_map/psum | solution.py:320
  (262 shorter events, 48.0 us)
Async XLA Ops:
  7.2 41.3 %all-gather.9.cloned.1.call-start = ((), (), s32[]{:S(2)}) async-start(), calls=%async_computation.8 | async-start | bytes 1638400 | tf_op jit(solution)/shard_map/all_gather | solution.py:61
  7.9 78.1 %all-gather.21.cloned.1.call-start = ((), (), s32[]{:S(2)}) async-start(), calls=%async_computation.22 | async-start | bytes 2359296 | tf_op jit(solution)/shard_map/all_gather | solution.py:141
  11.9 30.6 %copy-start.51 = (f32[4,128]{1,0:T(4,128)}, f32[4,128]{1,0:T(4,128)S(1)}, u32[]{:S(2)}) copy-start(f32[4,128]{1,0:T(4,128)S(1)} %fusion.58) | copy-start | bytes 6148
  11.9 20.5 %copy-start.47 = (f32[512]{0:T(512)}, f32[512]{0:T(512)S(1)}, u32[]{:S(2)}) copy-start(f32[512]{0:T(512)S(1)} %bitcast_rsqrt_fusion.1) | copy-start | bytes 6148
  26.2 9.1 %copy-start.56 = (f32[256]{0:T(256)}, f32[256]{0:T(256)S(1)}, u32[]{:S(2)}) copy-start(f32[256]{0:T(256)S(1)} %convert_add_fusion.6) | copy-start | bytes 3076
  32.4 3.0 copy-start.20
  32.4 10.0 %copy-start.42 = (f32[640]{0:T(1024)}, f32[640]{0:T(1024)S(1)}, u32[]{:S(2)}) copy-start(f32[640]{0:T(1024)S(1)} %convert_add_fusion.4) | copy-start | bytes 7684
  33.9 2.4 copy-start.44
  33.9 8.6 copy-start.3
  34.7 19.6 %copy-start.25 = (f32[128,128]{1,0:T(8,128)}, f32[128,128]{1,0:T(8,128)S(1)}, u32[]{:S(2)}) copy-start(f32[128,128]{1,0:T(8,128)S(1)} %get-tuple-element.348) | copy-start | bytes 196612
  34.7 19.6 %copy-start.27 = (f32[128,128]{1,0:T(8,128)}, f32[128,128]{1,0:T(8,128)S(1)}, u32[]{:S(2)}) copy-start(f32[128,128]{1,0:T(8,128)S(1)} %get-tuple-element.349) | copy-start | bytes 196612
  36.2 100.4 %all-gather.11.cloned.1.call-start = ((), (), s32[]{:S(2)}) async-start(), calls=%async_computation.9 | async-start | bytes 2359296 | tf_op jit(solution)/shard_map/all_gather | solution.py:142
  42.5 3.1 copy-start.18
  42.7 8.2 copy-start.14
  42.7 3.7 copy-start.55
  43.9 110.9 %all-gather.13.cloned.1.call-start = ((), (), s32[]{:S(2)}) async-start(), calls=%async_computation.10 | async-start | bytes 1638400 | tf_op jit(solution)/shard_map/all_gather | solution.py:64
  44.4 137.3 %all-gather.15.cloned.1.call-start = ((), (), s32[]{:S(2)}) async-start(), calls=%async_computation.11 | async-start | bytes 3276800 | tf_op jit(solution)/shard_map/all_gather | solution.py:65
  45.0 163.7 %all-gather.17.cloned.1.call-start = ((), (), s32[]{:S(2)}) async-start(), calls=%async_computation.12 | async-start | bytes 3276800 | tf_op jit(solution)/shard_map/all_gather | solution.py:66
  45.6 190.3 %all-gather.19.cloned.1.call-start = ((), (), s32[]{:S(2)}) async-start(), calls=%async_computation.13 | async-start | bytes 3276800 | tf_op jit(solution)/shard_map/all_gather | solution.py:67
  46.4 302.3 %reduce-scatter.17.cloned.1.call-start = ((), (), s32[]{:S(2)}) async-start(), calls=%async_computation.18 | async-start | bytes 1638400 | tf_op jit(solution)/shard_map/reduce_scatter | solution.py:289
  46.4 7.5 copy-start.58
  86.0 6.6 copy-start.22
  89.4 3.3 copy-start.16
  154.7 2.8 copy-start.4
  235.9 4.4 copy-start.17
  235.9 7.1 copy-start.64
  235.9 7.1 copy-start.67
  241.6 2.0 copy-start.62
  243.0 5.4 copy-start.34
  243.6 4.9 copy-start.60
  248.4 1.9 copy-start.66
  248.4 2.1 copy-start.65
  248.5 3.2 copy-start.61
  251.7 2.1 copy-start.11
  254.7 1.9 copy-start.32
  270.2 84.1 %reduce-scatter.11.cloned.1.call-start = ((), (), s32[]{:S(2)}) async-start(), calls=%async_computation.15 | async-start | bytes 1638400 | tf_op jit(solution)/shard_map/reduce_scatter | solution.py:280
  278.6 2.2 copy-start.31
  278.6 2.3 copy-start.63
  298.6 2.1 copy-start.31
  298.6 2.2 copy-start.63
  318.0 1.8 copy-start.28
  319.8 2.2 copy-start.2
  319.8 2.2 copy-start.41
  319.8 2.2 copy-start.59
  323.5 2.1 copy-start.15
  325.6 2.0 copy-start.38
  327.6 63.9 %reduce-scatter.19.cloned.1.call-start = ((), (), s32[]{:S(2)}) async-start(), calls=%async_computation.19 | async-start | bytes 3276800 | tf_op jit(solution)/shard_map/reduce_scatter | solution.py:292
  332.3 96.6 %reduce-scatter.21.cloned.1.call-start = ((), (), s32[]{:S(2)}) async-start(), calls=%async_computation.20 | async-start | bytes 3276800 | tf_op jit(solution)/shard_map/reduce_scatter | solution.py:295
  337.3 128.8 %reduce-scatter.23.cloned.1.call-start = ((), (), s32[]{:S(2)}) async-start(), calls=%async_computation.21 | async-start | bytes 3276800 | tf_op jit(solution)/shard_map/reduce_scatter | solution.py:298
  343.3 276.2 %reduce-scatter.9.cloned.1.call-start = ((), (), s32[]{:S(2)}) async-start(), calls=%async_computation.14 | async-start | bytes 9437184 | tf_op jit(solution)/shard_map/reduce_scatter | solution.py:257
  343.3 2.0 copy-start.30
  344.0 297.9 %reduce-scatter.15.cloned.1.call-start = ((), (), s32[]{:S(2)}) async-start(), calls=%async_computation.17 | async-start | bytes 409600 | tf_op jit(solution)/shard_map/reduce_scatter | solution.py:286
  348.7 273.4 %copy-start.9 = (f32[512,256]{1,0:T(8,128)S(1)}, f32[512,256]{1,0:T(8,128)}, u32[]{:S(2)}) copy-start(f32[512,256]{1,0:T(8,128)} %copy-done.8) | copy-start | bytes 1572868
  348.7 273.4 %copy-start.50 = (f32[4,128]{1,0:T(4,128)S(1)}, f32[4,128]{1,0:T(4,128)}, u32[]{:S(2)}) copy-start(f32[4,128]{1,0:T(4,128)} %copy-done.49) | copy-start | bytes 6148
  348.7 273.4 %copy-start.57 = (f32[256]{0:T(256)S(1)}, f32[256]{0:T(256)}, u32[]{:S(2)}) copy-start(f32[256]{0:T(256)} %copy-done.56) | copy-start | bytes 3076
  622.0 43.4 %reduce-scatter.13.cloned.1.call-start = ((), (), s32[]{:S(2)}) async-start(), calls=%async_computation.16 | async-start | bytes 409600 | tf_op jit(solution)/shard_map/reduce_scatter | solution.py:283
  622.6 2.9 copy-start.5
  622.6 2.9 copy-start.19
  622.6 2.9 copy-start.43
  622.6 2.9 copy-start.48
  625.6 10.4 %copy-start.52 = (f32[4,128]{1,0:T(4,128)S(1)}, f32[4,128]{1,0:T(4,128)}, u32[]{:S(2)}) copy-start(f32[4,128]{1,0:T(4,128)} %copy-done.51) | copy-start | bytes 6148
  625.6 10.4 %copy-start.13 = (f32[512,640]{1,0:T(8,128)S(1)}, f32[512,640]{1,0:T(8,128)}, u32[]{:S(2)}) copy-start(f32[512,640]{1,0:T(8,128)} %copy-done.12) | copy-start | bytes 3932164
  635.7 29.7 %copy-start.36 = (bf16[160,2048]{1,0:T(8,128)(2,1)S(1)}, bf16[160,2048]{1,0:T(8,128)(2,1)}, u32[]{:S(2)}) copy-start(bf16[160,2048]{1,0:T(8,128)(2,1)} %reduce-scatter.19.cloned.1.call-done) | copy-start | bytes 1966084
  635.7 29.7 %copy-start.37 = (bf16[160,2048]{1,0:T(8,128)(2,1)S(1)}, bf16[160,2048]{1,0:T(8,128)(2,1)}, u32[]{:S(2)}) copy-start(bf16[160,2048]{1,0:T(8,128)(2,1)} %reduce-scatter.21.cloned.1.call-done) | copy-start | bytes 1966084
  (22 other events, 26.9 us)
Sparse Core Ops, SparseCore 0:
  9.6 21.7 all-gather.8
  36.3 49.7 all-gather.20
  88.8 47.7 all-gather.10
  138.0 16.6 all-gather.12
  156.1 25.5 all-gather.14
  183.1 25.5 all-gather.16
  210.3 25.5 all-gather.18
  270.3 26.5 reduce-scatter.16
  327.7 26.6 reduce-scatter.10
  356.7 34.6 reduce-scatter.18
  394.2 34.6 reduce-scatter.20
  431.3 34.6 reduce-scatter.22
  470.1 149.3 reduce-scatter.8
  622.4 19.4 reduce-scatter.14
  645.0 20.4 reduce-scatter.12
where the time goes:
time: 902 us; the launch traced here: 894 us
  waiting for transfers between devices  440 us (49%)
  blocking collectives  250 us (28%)
  matrix products  88.8 us (10%)
  local copies, waits for them, and re-layouts  62.2 us (7%)
  other arithmetic  33.9 us (4%)
  between operations  17.6 us (2%)
    psum x1, blocking collectives, body(): lax.psum((shards[0], shards[1], shards[2], shards[3], shards[4], shards[5...  222 us
    reduce_scatter x1, waiting for transfers between devices, body(): lax.psum_scatter(key_buffer, 'ctx', scatter_dimension=1, tiled=True)  153 us
    all_gather x1, waiting for transfers between devices, body(): value_piece = lax.all_gather(value_b, 'ctx', axis=1, tiled=True)  41.7 us
    reduce_scatter x1, waiting for transfers between devices, body(): lax.psum_scatter(grad_up.astype(jnp.bfloat16), 'fsdp', scatter_dimension=...  37.4 us
    reduce_scatter x1, waiting for transfers between devices, body(): lax.psum_scatter(grad_down.astype(jnp.bfloat16), 'fsdp', scatter_dimensio...  37.1 us
    reduce_scatter x1, waiting for transfers between devices, body(): lax.psum_scatter(grad_gate.astype(jnp.bfloat16), 'fsdp', scatter_dimensio...  37.1 us
    all_gather x1, waiting for transfers between devices, body(): key_piece = lax.all_gather(key_b, 'ctx', axis=1, tiled=True)  27.3 us
    unnamed x147, local copies, waits for them, and re-layouts  25.9 us
  transfers between devices with their start and end apart: 15, of which 13 were waited for; matrix products, arithmetic and copies ran while one was open for 15% of the time, Pallas kernels for 0%

commit v1 on v0

--- a/solution.py
+++ b/solution.py
@@ -138,7 +138,12 @@
 
     stat_shape = (seq_count, head_count, row_count)
     running_max = jnp.full(stat_shape, MASKED_SCORE, jnp.float32)
-    key_piece = lax.all_gather(key_b, "ctx", axis=1, tiled=True)
+    ring = [key_b]
+    for hop in range(7):
+        ring.append(lax.ppermute(ring[-1], "ctx", [(dev, (dev + 1) % 8) for dev in range(8)]))
+    key_piece = jnp.roll(
+        jnp.concatenate(ring[::-1], axis=1), (lax.axis_index("ctx") + 1) * ring[0].shape[1], axis=1
+    )
     value_piece = lax.all_gather(value_b, "ctx", axis=1, tiled=True)
     mask_now = allowed(jnp.int32(0), key_piece.shape[1])
     scores = jnp.where(mask_now, raw_scores(key_piece), MASKED_SCORE)

time: 902 us -> 877 us (0.972)
  waiting for transfers between devices: 440 us -> 394 us
  local copies, waits for them, and re-layouts: 62.2 us -> 75.8 us
    ppermute x0 -> x7, waiting for transfers between devices: none -> 79 us  [body(): lax.ppermute(ring[-1], 'ctx', [(dev, (dev + 1) % 8) for dev in range(8)])]
    all_gather x1, waiting for transfers between devices: 41.7 us -> 0.02 us  [body(): value_piece = lax.all_gather(value_b, 'ctx', axis=1, tiled=True)]
    all_gather x1, waiting for transfers between devices: 21.2 us -> 0.01 us  [body(): lax.all_gather(up_weight, 'fsdp', axis=0, tiled=True)]
    all_gather x1, waiting for transfers between devices: 21.1 us -> 0.01 us  [body(): lax.all_gather(gate_weight, 'fsdp', axis=0, tiled=True)]
    all_gather x1, waiting for transfers between devices: 18.9 us -> 1.2 us  [body(): lax.all_gather(down_weight, 'fsdp', axis=0, tiled=True)]
    unnamed x147 -> x177, local copies, waits for them, and re-layouts: 25.9 us -> 39.4 us
    all_gather x1, waiting for transfers between devices: 27.3 us -> 14.1 us  [body(): lax.all_gather(key_b, 'ctx', axis=1, tiled=True)]
  transfers between devices with their start and end apart: 15 -> 22, of which waited for: 13 -> 16; matrix products, arithmetic and copies ran while one was open for 15% -> 21% of each run, Pallas kernels for 0% -> 0%
where the time goes in v1:
time: 877 us; the launch traced here: 868 us
  waiting for transfers between devices  394 us (45%)
  blocking collectives  251 us (29%)
  matrix products  89.3 us (10%)
  local copies, waits for them, and re-layouts  75.8 us (9%)
  other arithmetic  37.2 us (4%)
  between operations  17.7 us (2%)
    psum x1, blocking collectives, body(): lax.psum((shards[0], shards[1], shards[2], shards[3], shards[4], shards[5...  222 us
    reduce_scatter x1, waiting for transfers between devices, body(): lax.psum_scatter(key_buffer, 'ctx', scatter_dimension=1, tiled=True)  154 us
    ppermute x7, waiting for transfers between devices, body(): lax.ppermute(ring[-1], 'ctx', [(dev, (dev + 1) % 8) for dev in range(8)])  79 us
    unnamed x177, local copies, waits for them, and re-layouts  39.4 us
    reduce_scatter x1, waiting for transfers between devices, body(): lax.psum_scatter(grad_up.astype(jnp.bfloat16), 'fsdp', scatter_dimension=...  37.4 us
    reduce_scatter x1, waiting for transfers between devices, body(): lax.psum_scatter(grad_down.astype(jnp.bfloat16), 'fsdp', scatter_dimensio...  37.1 us
    reduce_scatter x1, waiting for transfers between devices, body(): lax.psum_scatter(grad_gate.astype(jnp.bfloat16), 'fsdp', scatter_dimensio...  37.1 us
    reduce_scatter x1, waiting for transfers between devices, body(): lax.psum_scatter(grad_key.astype(jnp.bfloat16), 'fsdp', scatter_dimension...  23.5 us
  transfers between devices with their start and end apart: 22, of which 16 were waited for; matrix products, arithmetic and copies ran while one was open for 21% of the time, Pallas kernels for 0%

profile of v1, /device:TPU:0, one launch (start us, length us, event | category | flops | bytes accessed | tf_op | source)
XLA Modules:
  0.0 868.0 jit_solution(13763990951155789459)
XLA Ops:
  15.7 9.0 %all-reduce.18 = (bf16[256]{0:T(256)(128)(2,1)S(1)}, bf16[640]{0:T(1024)(128)(2,1)S(1)}, bf16[256]{0:T(256)(128)(2,1)S(1)}, bf16[640]{0:T(1024)(128)(2,1)S(1)}, ...) all-reduce(bf16[256]{0:T(256)(128)(2,1)S(1)} %dynamic-update-slice., ...), channel_id=1, replica_groups=mesh['ctx'=8,'fsdp'=4] {'fsdp'}, use_global_device_ids=true, to_apply=%add.5 | all-reduce | flops 3072 | bytes 12288
  24.7 7.1 all_gather.51
  38.2 6.2 all_gather.47
  48.5 15.2 %collective-permute-done = bf16[4,128,256]{2,1,0:T(8,128)(2,1)S(1)} collective-permute-done((bf16[4,128,256]{2,1,0:T(8,128)(2,1)S(1)}, bf16[4,128,256]{2,1,0:T(8,128)(2,1)S(1)}, u32[]{:S(2)}, u32[]{:S(2)}) %collective-permute-start) | collective-permute-done | bytes 262176 | tf_op jit(solution)/shard_map/ppermute | solution.py:143
  63.7 14.9 %collective-permute-done.1 = bf16[4,128,256]{2,1,0:T(8,128)(2,1)S(1)} collective-permute-done((bf16[4,128,256]{2,1,0:T(8,128)(2,1)S(1)}, bf16[4,128,256]{2,1,0:T(8,128)(2,1)S(1)}, u32[]{:S(2)}, u32[]{:S(2)}) %collective-permute-start.1) | collective-permute-done | bytes 262176 | tf_op jit(solution)/shard_map/ppermute | solution.py:143
  79.3 15.6 %collective-permute-done.2 = bf16[4,128,256]{2,1,0:T(8,128)(2,1)S(1)} collective-permute-done((bf16[4,128,256]{2,1,0:T(8,128)(2,1)S(1)}, bf16[4,128,256]{2,1,0:T(8,128)(2,1)S(1)}, u32[]{:S(2)}, u32[]{:S(2)}) %collective-permute-start.2) | collective-permute-done | bytes 262176 | tf_op jit(solution)/shard_map/ppermute | solution.py:143
  95.0 9.0 %collective-permute-done.3 = bf16[4,128,256]{2,1,0:T(8,128)(2,1)S(1)} collective-permute-done((bf16[4,128,256]{2,1,0:T(8,128)(2,1)S(1)}, bf16[4,128,256]{2,1,0:T(8,128)(2,1)S(1)}, u32[]{:S(2)}, u32[]{:S(2)}) %collective-permute-start.3) | collective-permute-done | bytes 262176 | tf_op jit(solution)/shard_map/ppermute | solution.py:143
  104.0 9.0 %collective-permute-done.4 = bf16[4,128,256]{2,1,0:T(8,128)(2,1)S(1)} collective-permute-done((bf16[4,128,256]{2,1,0:T(8,128)(2,1)S(1)}, bf16[4,128,256]{2,1,0:T(8,128)(2,1)S(1)}, u32[]{:S(2)}, u32[]{:S(2)}) %collective-permute-start.4) | collective-permute-done | bytes 262176 | tf_op jit(solution)/shard_map/ppermute | solution.py:143
  113.8 9.2 %collective-permute-done.5 = bf16[4,128,256]{2,1,0:T(8,128)(2,1)} collective-permute-done((bf16[4,128,256]{2,1,0:T(8,128)(2,1)S(1)}, bf16[4,128,256]{2,1,0:T(8,128)(2,1)}, u32[]{:S(2)}, u32[]{:S(2)}) %collective-permute-start.5) | collective-permute-done | bytes 262176 | tf_op jit(solution)/shard_map/ppermute | solution.py:143
  123.6 2.6 broadcast_and_fusion.1
  126.3 6.1 collective-permute-done.6
  132.4 1.7 constant_dynamic-update-slice_fusion.16
  134.0 1.7 constant_dynamic-update-slice_fusion.15
  135.7 1.7 constant_dynamic-update-slice_fusion.14
  141.1 1.7 constant_dynamic-update-slice_fusion.8
  142.8 1.7 constant_dynamic-update-slice_fusion.7
  148.9 2.4 copy.67
  151.3 2.5 multiply_reduce_fusion.3
  159.2 3.4 fusion.28
  162.6 2.3 fusion.29
  165.9 8.2 fusion.45
  176.1 2.8 multiply_reduce_fusion.10
  182.1 5.7 fusion.81
  187.8 8.3 multiply_convert_fusion.1
  197.3 4.4 multiply_reduce_fusion.8
  205.0 4.8 multiply_convert_fusion
  209.9 1.8 fusion.82
  213.1 2.1 multiply_reduce_fusion.4
  218.0 2.0 convolution_convert_fusion.5
  220.0 2.6 reshape.457
  222.7 2.4 copy.71
  225.1 3.7 convolution_convert_fusion.3
  228.7 2.8 bitcast_convert_fusion
  231.7 3.0 multiply_reduce_fusion
  234.7 14.1 %all-gather.21.cloned.1.call-done = bf16[4,1024,1,256]{3,1,0,2:T(8,128)(2,1)} async-done(((bf16[4,128,1,256]{3,1,0,2:T(8,128)(2,1)}), bf16[4,1024,1,256]{3,1,0,2:T(8,128)(2,1)}) %all-gather.21.cloned.1.call-update) | async-done | bytes 2097168 | tf_op jit(solution)/shard_map/all_gather | solution.py:234
  248.8 4.4 broadcast_in_dim.140.clone
  253.2 40.5 %while.16 = (s32[]{:T(128)}, f32[4,128,4,256]{1,3,2,0:T(8,128)S(1)}, f32[4,1024,512]{2,1,0:T(8,128)}, bf16[4,1024,256]{2,1,0:T(8,128)(2,1)}, s32[4]{0:T(128)S(1)...) while((s32[]{:T(128)}, ...), condition=%wide.region_12.13_spmd.clone, body=%wide.region_11.12_spmd.clone.sunk | while | flops 2698316288 | bytes 81694016 | solution.py:256
  254.2 2.3 fusion.152
  261.4 2.4 pad_maximum_fusion.5
  263.8 5.3 copy.128
  269.1 4.6 constant_dynamic-update-slice_fusion.18
  274.3 2.1 fusion.152
  281.3 2.4 pad_maximum_fusion.5
  283.7 5.3 copy.128
  289.0 4.7 constant_dynamic-update-slice_fusion.18
  293.7 1.8 copy.72
  295.5 2.0 multiply_add_fusion.1
  301.3 1.9 convolution_convert_fusion.4
  303.3 4.6 convolution_convert_fusion.2
  308.2 4.9 convolution_convert_fusion.1
  314.1 4.9 convolution_convert_fusion
  321.2 3.3 fusion.83
  324.5 4.0 reduce-scatter.11.cloned.1.call-done
  328.5 37.1 %reduce-scatter.19.cloned.1.call-done = bf16[160,2048]{1,0:T(8,128)(2,1)} async-done(((bf16[640,2048]{1,0:T(8,128)(2,1)}), bf16[160,2048]{1,0:T(8,128)(2,1)}) %reduce-scatter.19.cloned.1.call-update) | async-done | bytes 655376 | tf_op jit(solution)/shard_map/reduce_scatter | solution.py:297
  365.6 37.4 %reduce-scatter.21.cloned.1.call-done = bf16[160,2048]{1,0:T(8,128)(2,1)} async-done(((bf16[640,2048]{1,0:T(8,128)(2,1)}), bf16[160,2048]{1,0:T(8,128)(2,1)}) %reduce-scatter.21.cloned.1.call-update) | async-done | bytes 655376 | tf_op jit(solution)/shard_map/reduce_scatter | solution.py:300
  403.0 37.1 %reduce-scatter.23.cloned.1.call-done = bf16[512,640]{1,0:T(8,128)(2,1)} async-done(((bf16[2048,640]{1,0:T(8,128)(2,1)}), bf16[512,640]{1,0:T(8,128)(2,1)}) %reduce-scatter.23.cloned.1.call-update) | async-done | bytes 655376 | tf_op jit(solution)/shard_map/reduce_scatter | solution.py:303
  440.1 153.5 %reduce-scatter.9.cloned.1.call-done = f32[4,128,512]{2,1,0:T(8,128)} async-done(((f32[4,1024,512]{2,1,0:T(8,128)}), f32[4,128,512]{2,1,0:T(8,128)}) %reduce-scatter.9.cloned.1.call-update) | async-done | bytes 1048592 | tf_op jit(solution)/shard_map/reduce_scatter | solution.py:262
  596.8 1.8 convolution_add_fusion.1
  599.7 1.6 fusion.58
  601.4 7.1 all-reduce.17
  610.1 2.7 fusion.53
  612.7 3.3 reduce-scatter.15.cloned.1.call-done
  616.0 23.5 %reduce-scatter.13.cloned.1.call-done = bf16[160,256]{1,0:T(8,128)(2,1)} async-done(((bf16[640,256]{1,0:T(8,128)(2,1)}), bf16[160,256]{1,0:T(8,128)(2,1)}) %reduce-scatter.13.cloned.1.call-update) | async-done | bytes 81936 | tf_op jit(solution)/shard_map/reduce_scatter | solution.py:288
  639.6 221.7 %all-reduce.20 = (f32[160,1024]{1,0:T(8,128)}, f32[160,256]{1,0:T(8,128)}, f32[160,256]{1,0:T(8,128)}, f32[256,640]{1,0:T(8,128)}, f32[160,2048]{1,0:T(8,128)}, ...) all-reduce(bf16[160,1024]{1,0:T(8,128)(2,1)} %reduce-scatter.11.clo, ...), channel_id=1, replica_groups=mesh['ctx'=8,'fsdp'=4] {'ctx'}, use_global_device_ids=true, to_apply=%region_18.19 | all-reduce | flops 1393408 | bytes 8361984 | tf_op jit(solution)/shard_map/psum | solution.py:325
  (308 shorter events, 70.1 us)
Async XLA Ops:
  7.2 141.7 %all-gather.9.cloned.1.call-start = ((), (), s32[]{:S(2)}) async-start(), calls=%async_computation.8 | async-start | bytes 1638400 | tf_op jit(solution)/shard_map/all_gather | solution.py:61
  7.9 158.0 %all-gather.11.cloned.1.call-start = ((), (), s32[]{:S(2)}) async-start(), calls=%async_computation.9 | async-start | bytes 2359296 | tf_op jit(solution)/shard_map/all_gather | solution.py:147
  31.7 5.2 copy-start.18
  33.1 11.3 %copy-start.58 = (f32[4,128]{1,0:T(4,128)}, f32[4,128]{1,0:T(4,128)S(1)}, u32[]{:S(2)}) copy-start(f32[4,128]{1,0:T(4,128)S(1)} %fusion.59) | copy-start | bytes 6148
  33.2 11.3 %copy-start.49 = (f32[640]{0:T(1024)}, f32[640]{0:T(1024)S(1)}, u32[]{:S(2)}) copy-start(f32[640]{0:T(1024)S(1)} %convert_add_fusion.4) | copy-start | bytes 7684
  34.5 116.8 %copy-start.14 = (bf16[4,128,640]{2,1,0:T(8,128)(2,1)}, bf16[4,128,640]{2,1,0:T(8,128)(2,1)S(1)}, u32[]{:S(2)}) copy-start(bf16[4,128,640]{2,1,0:T(8,128)(2,1)S(1)} %fusion.61) | copy-start | bytes 1966084
  34.5 3.7 copy-start.51
  34.5 10.0 %copy-start.3 = (bf16[4,128,640]{2,1,0:T(8,128)(2,1)S(1)}, bf16[4,128,640]{2,1,0:T(8,128)(2,1)}, u32[]{:S(2)}) copy-start(bf16[4,128,640]{2,1,0:T(8,128)(2,1)} %param.18) | copy-start | bytes 1966084
  35.6 140.4 %all-gather.13.cloned.1.call-start = ((), (), s32[]{:S(2)}) async-start(), calls=%async_computation.10 | async-start | bytes 1638400 | tf_op jit(solution)/shard_map/all_gather | solution.py:64
  36.4 145.7 %all-gather.15.cloned.1.call-start = ((), (), s32[]{:S(2)}) async-start(), calls=%async_computation.11 | async-start | bytes 3276800 | tf_op jit(solution)/shard_map/all_gather | solution.py:65
  37.0 150.8 %all-gather.17.cloned.1.call-start = ((), (), s32[]{:S(2)}) async-start(), calls=%async_computation.12 | async-start | bytes 3276800 | tf_op jit(solution)/shard_map/all_gather | solution.py:66
  37.6 159.8 %all-gather.19.cloned.1.call-start = ((), (), s32[]{:S(2)}) async-start(), calls=%async_computation.13 | async-start | bytes 3276800 | tf_op jit(solution)/shard_map/all_gather | solution.py:67
  38.1 210.7 %all-gather.21.cloned.1.call-start = ((), (), s32[]{:S(2)}) async-start(), calls=%async_computation.22 | async-start | bytes 2359296 | tf_op jit(solution)/shard_map/all_gather | solution.py:234
  44.7 68.3 %copy-start.62 = (s32[4]{0:T(128)S(1)}, s32[4]{0:T(128)}, u32[]{:S(2)}) copy-start(s32[4]{0:T(128)} %param.20) | copy-start | bytes 52
  45.2 78.3 %copy-start.60 = (f32[512]{0:T(512)}, f32[512]{0:T(512)S(1)}, u32[]{:S(2)}) copy-start(f32[512]{0:T(512)S(1)} %get-tuple-element.354) | copy-start | bytes 6148
  45.2 78.3 %copy-start.56 = (f32[4,128]{1,0:T(4,128)}, f32[4,128]{1,0:T(4,128)S(1)}, u32[]{:S(2)}) copy-start(f32[4,128]{1,0:T(4,128)S(1)} %bitcast_rsqrt_fusion) | copy-start | bytes 6148
  45.6 108.7 %copy-start.25 = (f32[128,128]{1,0:T(8,128)}, f32[128,128]{1,0:T(8,128)S(1)}, u32[]{:S(2)}) copy-start(f32[128,128]{1,0:T(8,128)S(1)} %get-tuple-element.350) | copy-start | bytes 196612
  45.6 108.7 %copy-start.27 = (f32[128,128]{1,0:T(8,128)}, f32[128,128]{1,0:T(8,128)S(1)}, u32[]{:S(2)}) copy-start(f32[128,128]{1,0:T(8,128)S(1)} %get-tuple-element.351) | copy-start | bytes 196612
  47.0 16.7 %collective-permute-start = (bf16[4,128,256]{2,1,0:T(8,128)(2,1)S(1)}, bf16[4,128,256]{2,1,0:T(8,128)(2,1)S(1)}, u32[]{:S(2)}, u32[]{:S(2)}) collective-permute-start(bf16[4,128,256]{2,1,0:T(8,128)(2,1)S(1)} %get-tuple-element.349), channel_id=1, source_target_pairs={{0,4},{4,8},{8,12},{12,16},{16,20},{20,24},{24,28},{28,0},{1,5},{5... | collective-permute-start | bytes 786440 | tf_op jit(solution)/shard_map/ppermute | solution.py:143
  63.7 14.9 %collective-permute-start.1 = (bf16[4,128,256]{2,1,0:T(8,128)(2,1)S(1)}, bf16[4,128,256]{2,1,0:T(8,128)(2,1)S(1)}, u32[]{:S(2)}, u32[]{:S(2)}) collective-permute-start(bf16[4,128,256]{2,1,0:T(8,128)(2,1)S(1)} %collective-permute-done), channel_id=1, source_target_pairs={{0,4},{4,8},{8,12},{12,16},{16,20},{20,24},{24,28},{28,0},{1,5},{5... | collective-permute-start | bytes 786440 | tf_op jit(solution)/shard_map/ppermute | solution.py:143
  79.3 15.6 %collective-permute-start.2 = (bf16[4,128,256]{2,1,0:T(8,128)(2,1)S(1)}, bf16[4,128,256]{2,1,0:T(8,128)(2,1)S(1)}, u32[]{:S(2)}, u32[]{:S(2)}) collective-permute-start(bf16[4,128,256]{2,1,0:T(8,128)(2,1)S(1)} %collective-permute-done.1), channel_id=1, source_target_pairs={{0,4},{4,8},{8,12},{12,16},{16,20},{20,24},{24,28},{28,0},{1,5},{5... | collective-permute-start | bytes 786440 | tf_op jit(solution)/shard_map/ppermute | solution.py:143
  94.9 28.7 %copy-start.35 = (bf16[4,128,256]{2,1,0:T(8,128)(2,1)}, bf16[4,128,256]{2,1,0:T(8,128)(2,1)S(1)}, u32[]{:S(2)}) copy-start(bf16[4,128,256]{2,1,0:T(8,128)(2,1)S(1)} %collective-permute-done.2) | copy-start | bytes 786436
  94.9 9.1 %collective-permute-start.3 = (bf16[4,128,256]{2,1,0:T(8,128)(2,1)S(1)}, bf16[4,128,256]{2,1,0:T(8,128)(2,1)S(1)}, u32[]{:S(2)}, u32[]{:S(2)}) collective-permute-start(bf16[4,128,256]{2,1,0:T(8,128)(2,1)S(1)} %collective-permute-done.2), channel_id=1, source_target_pairs={{0,4},{4,8},{8,12},{12,16},{16,20},{20,24},{24,28},{28,0},{1,5},{5... | collective-permute-start | bytes 786440 | tf_op jit(solution)/shard_map/ppermute | solution.py:143
  94.9 229.5 %reduce-scatter.17.cloned.1.call-start = ((), (), s32[]{:S(2)}) async-start(), calls=%async_computation.18 | async-start | bytes 1638400 | tf_op jit(solution)/shard_map/reduce_scatter | solution.py:294
  104.0 19.6 %copy-start.37 = (bf16[4,128,256]{2,1,0:T(8,128)(2,1)}, bf16[4,128,256]{2,1,0:T(8,128)(2,1)S(1)}, u32[]{:S(2)}) copy-start(bf16[4,128,256]{2,1,0:T(8,128)(2,1)S(1)} %collective-permute-done.3) | copy-start | bytes 786436
  104.0 9.1 %collective-permute-start.4 = (bf16[4,128,256]{2,1,0:T(8,128)(2,1)S(1)}, bf16[4,128,256]{2,1,0:T(8,128)(2,1)S(1)}, u32[]{:S(2)}, u32[]{:S(2)}) collective-permute-start(bf16[4,128,256]{2,1,0:T(8,128)(2,1)S(1)} %collective-permute-done.3), channel_id=1, source_target_pairs={{0,4},{4,8},{8,12},{12,16},{16,20},{20,24},{24,28},{28,0},{1,5},{5... | collective-permute-start | bytes 786440 | tf_op jit(solution)/shard_map/ppermute | solution.py:143
  113.0 10.5 %copy-start.39 = (bf16[4,128,256]{2,1,0:T(8,128)(2,1)}, bf16[4,128,256]{2,1,0:T(8,128)(2,1)S(1)}, u32[]{:S(2)}) copy-start(bf16[4,128,256]{2,1,0:T(8,128)(2,1)S(1)} %collective-permute-done.4) | copy-start | bytes 786436
  113.0 9.9 %collective-permute-start.5 = (bf16[4,128,256]{2,1,0:T(8,128)(2,1)S(1)}, bf16[4,128,256]{2,1,0:T(8,128)(2,1)}, u32[]{:S(2)}, u32[]{:S(2)}) collective-permute-start(bf16[4,128,256]{2,1,0:T(8,128)(2,1)S(1)} %collective-permute-done.4), channel_id=1, source_target_pairs={{0,4},{4,8},{8,12},{12,16},{16,20},{20,24},{24,28},{28,0},{1,5},{5... | collective-permute-start | bytes 786440 | tf_op jit(solution)/shard_map/ppermute | solution.py:143
  123.0 9.4 %collective-permute-start.6 = (bf16[4,128,256]{2,1,0:T(8,128)(2,1)}, bf16[4,128,256]{2,1,0:T(8,128)(2,1)}, u32[]{:S(2)}, u32[]{:S(2)}) collective-permute-start(bf16[4,128,256]{2,1,0:T(8,128)(2,1)} %collective-permute-done.5), channel_id=1, source_target_pairs={{0,4},{4,8},{8,12},{12,16},{16,20},{20,24},{24,28},{28,0},{1,5},{5... | collective-permute-start | bytes 786440 | tf_op jit(solution)/shard_map/ppermute | solution.py:143
  123.6 13.9 %copy-start.38 = (bf16[4,128,256]{2,1,0:T(8,128)(2,1)S(1)}, bf16[4,128,256]{2,1,0:T(8,128)(2,1)}, u32[]{:S(2)}) copy-start(bf16[4,128,256]{2,1,0:T(8,128)(2,1)} %copy-done.37) | copy-start | bytes 786436
  123.6 14.6 %copy-start.36 = (bf16[4,128,256]{2,1,0:T(8,128)(2,1)S(1)}, bf16[4,128,256]{2,1,0:T(8,128)(2,1)}, u32[]{:S(2)}) copy-start(bf16[4,128,256]{2,1,0:T(8,128)(2,1)} %copy-done.35) | copy-start | bytes 786436
  123.6 15.3 %copy-start.34 = (bf16[4,128,256]{2,1,0:T(8,128)(2,1)S(1)}, bf16[4,128,256]{2,1,0:T(8,128)(2,1)}, u32[]{:S(2)}) copy-start(bf16[4,128,256]{2,1,0:T(8,128)(2,1)} %copy-done.33) | copy-start | bytes 786436
  135.7 8.8 %copy-start.40 = (bf16[4,128,256]{2,1,0:T(8,128)(2,1)S(1)}, bf16[4,128,256]{2,1,0:T(8,128)(2,1)}, u32[]{:S(2)}) copy-start(bf16[4,128,256]{2,1,0:T(8,128)(2,1)} %copy-done.39) | copy-start | bytes 786436
  151.3 2.6 copy-start.65
  159.2 3.4 copy-start.22
  162.6 3.3 copy-start.16
  176.1 2.9 copy-start.4
  197.3 4.4 copy-start.17
  197.3 7.1 copy-start.72
  197.3 7.1 copy-start.75
  204.4 5.4 copy-start.41
  205.0 4.9 copy-start.67
  209.9 3.2 copy-start.68
  231.6 96.9 %reduce-scatter.11.cloned.1.call-start = ((), (), s32[]{:S(2)}) async-start(), calls=%async_computation.15 | async-start | bytes 1638400 | tf_op jit(solution)/shard_map/reduce_scatter | solution.py:285
  254.2 2.3 copy-start.31
  254.2 2.4 copy-start.70
  274.3 2.2 copy-start.70
  303.2 62.4 %reduce-scatter.19.cloned.1.call-start = ((), (), s32[]{:S(2)}) async-start(), calls=%async_computation.19 | async-start | bytes 3276800 | tf_op jit(solution)/shard_map/reduce_scatter | solution.py:297
  307.9 95.1 %reduce-scatter.21.cloned.1.call-start = ((), (), s32[]{:S(2)}) async-start(), calls=%async_computation.20 | async-start | bytes 3276800 | tf_op jit(solution)/shard_map/reduce_scatter | solution.py:300
  313.1 127.1 %reduce-scatter.23.cloned.1.call-start = ((), (), s32[]{:S(2)}) async-start(), calls=%async_computation.21 | async-start | bytes 3276800 | tf_op jit(solution)/shard_map/reduce_scatter | solution.py:303
  319.1 274.6 %reduce-scatter.9.cloned.1.call-start = ((), (), s32[]{:S(2)}) async-start(), calls=%async_computation.14 | async-start | bytes 9437184 | tf_op jit(solution)/shard_map/reduce_scatter | solution.py:262
  319.8 296.2 %reduce-scatter.15.cloned.1.call-start = ((), (), s32[]{:S(2)}) async-start(), calls=%async_computation.17 | async-start | bytes 409600 | tf_op jit(solution)/shard_map/reduce_scatter | solution.py:291
  324.5 271.8 %copy-start.9 = (f32[512,256]{1,0:T(8,128)S(1)}, f32[512,256]{1,0:T(8,128)}, u32[]{:S(2)}) copy-start(f32[512,256]{1,0:T(8,128)} %copy-done.8) | copy-start | bytes 1572868
  324.5 271.8 %copy-start.57 = (f32[4,128]{1,0:T(4,128)S(1)}, f32[4,128]{1,0:T(4,128)}, u32[]{:S(2)}) copy-start(f32[4,128]{1,0:T(4,128)} %copy-done.56) | copy-start | bytes 6148
  324.5 271.8 %copy-start.64 = (f32[256]{0:T(256)S(1)}, f32[256]{0:T(256)}, u32[]{:S(2)}) copy-start(f32[256]{0:T(256)} %copy-done.63) | copy-start | bytes 3076
  596.2 43.4 %reduce-scatter.13.cloned.1.call-start = ((), (), s32[]{:S(2)}) async-start(), calls=%async_computation.16 | async-start | bytes 409600 | tf_op jit(solution)/shard_map/reduce_scatter | solution.py:288
  596.7 2.9 copy-start.5
  596.8 2.9 copy-start.19
  596.8 2.9 copy-start.50
  596.8 2.9 copy-start.55
  599.7 10.3 %copy-start.59 = (f32[4,128]{1,0:T(4,128)S(1)}, f32[4,128]{1,0:T(4,128)}, u32[]{:S(2)}) copy-start(f32[4,128]{1,0:T(4,128)} %copy-done.58) | copy-start | bytes 6148
  599.7 10.3 %copy-start.13 = (f32[512,640]{1,0:T(8,128)S(1)}, f32[512,640]{1,0:T(8,128)}, u32[]{:S(2)}) copy-start(f32[512,640]{1,0:T(8,128)} %copy-done.12) | copy-start | bytes 3932164
  609.9 29.7 %copy-start.43 = (bf16[160,2048]{1,0:T(8,128)(2,1)S(1)}, bf16[160,2048]{1,0:T(8,128)(2,1)}, u32[]{:S(2)}) copy-start(bf16[160,2048]{1,0:T(8,128)(2,1)} %reduce-scatter.19.cloned.1.call-done) | copy-start | bytes 1966084
  609.9 29.7 %copy-start.44 = (bf16[160,2048]{1,0:T(8,128)(2,1)S(1)}, bf16[160,2048]{1,0:T(8,128)(2,1)}, u32[]{:S(2)}) copy-start(bf16[160,2048]{1,0:T(8,128)(2,1)} %reduce-scatter.21.cloned.1.call-done) | copy-start | bytes 1966084
  (37 other events, 57.4 us)
Sparse Core Ops, SparseCore 0:
  9.6 22.3 all-gather.8
  35.8 59.6 all-gather.10
  97.1 19.1 all-gather.12
  117.7 25.5 all-gather.14
  144.7 25.5 all-gather.16
  171.7 25.5 all-gather.18
  199.5 49.2 all-gather.20
  251.3 25.0 reduce-scatter.16
  303.4 25.1 reduce-scatter.10
  330.9 34.6 reduce-scatter.18
  368.3 34.6 reduce-scatter.20
  405.4 34.6 reduce-scatter.22
  444.2 149.3 reduce-scatter.8
  596.6 19.4 reduce-scatter.14
  619.1 20.4 reduce-scatter.12
